TPU v7x, 128 devices: a whole 4x4x4 slice. The times are simulated.
128 devices in a mesh: rows: 32 (over x, z, core), cols: 4 (over y).
Axes of the slice: x: 4, y: 4, z: 4, core: 2. Of those that a mesh axis runs over, the one named last changes fastest.
Arguments:
- gradient: bfloat16 [26624, 8192], P('rows', 'cols'), may hold values from -36 to 36
- momentum: float32 [26624, 8192], P('rows', 'cols'), may hold values from -6 to 6
- right_factor: float32 [8192, 512], P('cols'), may hold values from -0.0625 to 0.0625
Outputs:
- new_momentum: float32 [26624, 8192], P('rows', 'cols')
- new_factor: float32 [8192, 512], P('cols')
- left_basis: float32 [26624, 512], P('rows')
All inputs are finite; a program needn't handle non-finite values.
Results may differ from a plain program's by a relative error of at most 0.0003.
Values sent between devices are 32-bit elements; how exact they have to be, the bound alone decides.
A program may use at most 128 MiB of HBM per device.

v0:
```python
import jax
import jax.numpy as jnp
from jax import lax
from jax.sharding import PartitionSpec as P

momentum_decay = 0.95
norm_eps = 1e-06


def partner(shard, axis, apart):
    return lax.ppermute(shard, axis, [(i, i ^ 1 << apart) for i in range(lax.axis_size(axis))])


def exact_dot(left_arr, right_arr, dims):
    return lax.dot_general(
        left_arr,
        right_arr,
        (dims, ((), ())),
        precision=lax.Precision.HIGHEST,
        preferred_element_type=jnp.float32,
    )


def body(gradient, momentum, right_factor):
    blended = momentum + gradient.astype(jnp.float32)
    rank_width = right_factor.shape[1]
    part_rows = lax.psum(exact_dot(blended, right_factor, ((1,), (0,))), "cols")
    gram_local = exact_dot(part_rows, part_rows, ((0,), (0,)))
    gram_whole = gram_local
    for section_bit in range(lax.axis_size("rows").bit_length() - 1):
        gram_whole = gram_whole + partner(gram_whole, "rows", section_bit)
    lower_factor = jnp.linalg.cholesky(gram_whole)
    inverse = lax.linalg.triangular_solve(
        lower_factor, jnp.eye(rank_width, dtype=lower_factor.dtype), left_side=True, lower=True
    )
    left_basis = exact_dot(part_rows, inverse, ((1,), (1,)))
    summed = lax.psum(exact_dot(blended, left_basis, ((0,), (0,))), "rows")
    col_squares = lax.psum(jnp.sum(summed * summed, axis=0), "cols")
    new_factor = summed * lax.rsqrt(col_squares + norm_eps)
    new_momentum = blended - (1.0 - momentum_decay) * exact_dot(left_basis, summed, ((1,), (1,)))
    return (new_momentum, new_factor, left_basis)


def solution(mesh):
    return jax.shard_map(
        body,
        mesh=mesh,
        in_specs=(P("rows", "cols"), P("rows", "cols"), P("cols", None)),
        out_specs=(P("rows", "cols"), P("cols", None), P("rows", None)),
        check_vma=False,
    )
```

profile of v0, /device:TPU:6, one launch (start us, length us, event | category | flops | bytes accessed | tf_op | source)
XLA Modules:
  0.0 511.5 jit_solution(15978207523322824294)
XLA Ops:
  7.2 15.5 %fusion.1 = f32[832,512]{1,0:T(8,128)} fusion(f32[2048,512]{1,0:T(8,128)} %param.5, f32[832,2048]{1,0:T(8,128)} %param.4, bf16[832,2048]{1,0:T(8,128)(2,1)} %param.3), kind=kOutput, calls=%fused_computation.6 | convolution fusion | flops 10472390656 | bytes 16121856 | tf_op jit(solution)/shard_map/dot_general | solution.py:15
  22.8 54.7 %all-reduce.4.cloned.1.call-done = f32[832,512]{1,0:T(8,128)} async-done(((f32[832,512]{1,0:T(8,128)}), f32[832,512]{1,0:T(8,128)}) %all-reduce.4.cloned.1.call-update) | async-done | bytes 1703952 | tf_op jit(solution)/shard_map/psum | solution.py:27
  77.5 5.5 %fusion.48 = f32[512,512]{0,1:T(8,128)S(1)} fusion(f32[832,512]{1,0:T(8,128)} %all-reduce.4.cloned.1.call-done), kind=kOutput, calls=%fused_computation.87 | convolution fusion | flops 2617245696 | bytes 2752512 | tf_op jit(solution)/shard_map/dot_general | solution.py:15
  83.1 2.6 collective-permute-done
  86.0 1.6 collective-permute-start.1
  87.6 23.6 %collective-permute-done.1 = f32[512,512]{0,1:T(8,128)S(1)} collective-permute-done((f32[512,512]{0,1:T(8,128)S(1)}, f32[512,512]{0,1:T(8,128)S(1)}, u32[]{:S(2)}, u32[]{:S(2)}) %collective-permute-start.1) | collective-permute-done | bytes 1048608 | tf_op jit(solution)/shard_map/ppermute | solution.py:11
  111.4 3.2 collective-permute-start.2
  114.7 22.7 %collective-permute-done.2 = f32[512,512]{0,1:T(8,128)S(1)} collective-permute-done((f32[512,512]{0,1:T(8,128)S(1)}, f32[512,512]{0,1:T(8,128)S(1)}, u32[]{:S(2)}, u32[]{:S(2)}) %collective-permute-start.2) | collective-permute-done | bytes 1048608 | tf_op jit(solution)/shard_map/ppermute | solution.py:11
  137.6 0.9 collective-permute-start.3
  138.5 22.6 %collective-permute-done.3 = f32[512,512]{0,1:T(8,128)S(1)} collective-permute-done((f32[512,512]{0,1:T(8,128)S(1)}, f32[512,512]{0,1:T(8,128)S(1)}, u32[]{:S(2)}, u32[]{:S(2)}) %collective-permute-start.3) | collective-permute-done | bytes 1048608 | tf_op jit(solution)/shard_map/ppermute | solution.py:11
  161.4 1.7 collective-permute-start.4
  163.2 1.1 fusion.19
  164.2 21.4 %collective-permute-done.4 = f32[512,512]{0,1:T(8,128)S(1)} collective-permute-done((f32[512,512]{0,1:T(8,128)S(1)}, f32[512,512]{0,1:T(8,128)S(1)}, u32[]{:S(2)}, u32[]{:S(2)}) %collective-permute-start.4) | collective-permute-done | bytes 1048608 | tf_op jit(solution)/shard_map/ppermute | solution.py:11
  186.5 11.7 %cholesky.104 = f32[128,128]{1,0:T(8,128)S(1)} custom-call(f32[128,128]{1,0:T(8,128)S(1)} %cholesky.266), custom_call_target="Cholesky" | custom-call | tf_op jit(solution)/shard_map/jit(cholesky)/cholesky | solution.py:32
  198.2 9.8 %custom-call.30 = f32[1,128,128]{1,2,0:T(8,128)S(1)} custom-call(f32[1,128,128]{2,1,0:T(8,128)S(1)} %get-tuple-element.30), custom_call_target="InvertDiagBlocksLowerTriangular" | custom-call | tf_op jit(solution)/shard_map/jit(cholesky)/cholesky | solution.py:32
  208.0 1.1 cholesky.224
  209.1 1.0 constant_dynamic-update-slice_fusion.3
  210.5 11.7 %cholesky.217 = f32[128,128]{1,0:T(8,128)S(1)} custom-call(f32[128,128]{1,0:T(8,128)S(1)} %cholesky.270), custom_call_target="Cholesky" | custom-call | tf_op jit(solution)/shard_map/jit(cholesky)/cholesky | solution.py:32
  222.2 0.6 select_reduce_fusion.2
  222.8 10.0 %custom-call.31 = f32[1,128,128]{1,2,0:T(8,128)S(1)} custom-call(f32[1,128,128]{2,1,0:T(8,128)S(1)} %get-tuple-element.27), custom_call_target="InvertDiagBlocksLowerTriangular" | custom-call | tf_op jit(solution)/shard_map/jit(cholesky)/cholesky | solution.py:32
  232.8 0.9 convolution_dynamic-update-slice_fusion
  233.7 1.6 slice_subtract_fusion.1
  235.3 11.7 %cholesky.238 = f32[128,128]{1,0:T(8,128)S(1)} custom-call(f32[128,128]{1,0:T(8,128)S(1)} %cholesky.275), custom_call_target="Cholesky" | custom-call | tf_op jit(solution)/shard_map/jit(cholesky)/cholesky | solution.py:32
  247.7 0.7 compare_reduce_fusion.1
  248.4 9.8 %custom-call.32 = f32[1,128,128]{1,2,0:T(8,128)S(1)} custom-call(f32[1,128,128]{2,1,0:T(8,128)S(1)} %get-tuple-element.24), custom_call_target="InvertDiagBlocksLowerTriangular" | custom-call | tf_op jit(solution)/shard_map/jit(cholesky)/cholesky | solution.py:32
  258.2 0.8 convolution_dynamic-update-slice_fusion.1
  259.0 1.4 slice_subtract_fusion.2
  260.4 12.1 %cholesky.255 = f32[128,128]{1,0:T(8,128)S(1)} custom-call(f32[128,128]{1,0:T(8,128)S(1)} %slice_subtract_fusion.2), custom_call_target="Cholesky" | custom-call | tf_op jit(solution)/shard_map/jit(cholesky)/cholesky | solution.py:32
  273.2 0.7 compare_reduce_fusion
  273.8 0.7 compare_reduce_fusion.2
  277.1 2.3 select_select_fusion
  279.4 14.1 %while.1 = (s32[]{:T(128)}, f32[512,512]{1,0:T(8,128)}, s32[4,2]{0,1:T(2,128)S(1)}, f32[4,128,128]{2,1,0:T(8,128)}, s32[]{:T(128)}) while((s32[]{:T(128)}, f32[512,512]{1,0:T(8,128)}, s32[4,2]{0,1:T(2,128)S(1)}, f32[4,128,128]{2,1,0:T(8,128)}, s32[]{:T(128)}) %tuple.31), condition=%wide.while_cond, body=%wide.while_body.sunk | while | flops 2 | bytes 132205 | solution.py:33
  280.1 2.9 bitcast_dynamic-update-slice_fusion.2
  283.6 2.9 bitcast_dynamic-update-slice_fusion.2
  287.1 2.9 bitcast_dynamic-update-slice_fusion.2
  290.7 2.8 bitcast_dynamic-update-slice_fusion.2
  293.5 40.1 %custom-call.33 = f32[4,128,128]{1,2,0:T(8,128)S(1)} custom-call(f32[4,128,128]{2,1,0:T(8,128)} %get-tuple-element.10), custom_call_target="InvertDiagBlocksLowerTriangular" | custom-call | tf_op jit(solution)/shard_map/triangular_solve | solution.py:33
  334.0 1.5 convolution_subtract_fusion.1
  336.0 1.6 convolution_subtract_fusion
  338.0 2.0 convolution_subtract_fusion.2
  340.4 2.9 fusion.2
  343.3 1.2 copy-done.3
  344.5 15.1 %fusion = f32[2048,512]{1,0:T(8,128)} fusion(f32[832,512]{1,0:T(8,128)S(1)} %fusion.2, f32[832,2048]{1,0:T(8,128)S(1)} %bitcast.56, bf16[832,2048]{1,0:T(8,128)(2,1)S(1)} %copy-done.1), kind=kOutput, calls=%fused_computation.5 | convolution fusion | flops 10472390656 | bytes 16121856 | tf_op jit(solution)/shard_map/dot_general | solution.py:15
  359.7 112.6 %all-reduce.6.cloned.1.call-done = f32[2048,512]{1,0:T(8,128)} async-done(((f32[2048,512]{1,0:T(8,128)}), f32[2048,512]{1,0:T(8,128)}) %all-reduce.6.cloned.1.call-update) | async-done | bytes 4194320 | tf_op jit(solution)/shard_map/psum | solution.py:37
  472.2 2.5 multiply_reduce_fusion
  474.8 10.7 %psum.23 = f32[512]{0:T(512)S(1)} all-reduce(f32[512]{0:T(512)S(1)} %multiply_reduce_fusion), channel_id=1, replica_groups=mesh['rows'=32,'cols'=4] {'cols'}, use_global_device_ids=true, to_apply=%region_11.12 | all-reduce | flops 512 | bytes 4096 | tf_op jit(solution)/shard_map/psum | solution.py:38
  485.5 16.5 %multiply_subtract_fusion = f32[832,2048]{1,0:T(8,128)} fusion(f32[832,512]{1,0:T(8,128)} %copy-done.3, f32[2048,512]{1,0:T(8,128)} %all-reduce.6.cloned.1.call-done, f32[832,2048]{1,0:T(8,128)} %param.4, bf16[832,2048]{1,0:T(8,128)(2,1)S(1)} %copy-done.2), kind=kOutput, calls=%fused_computation.2 | convolution fusion | flops 10475798528 | bytes 22937600 | tf_op jit(solution)/shard_map/dot_general | solution.py:15
  501.9 2.5 broadcast_multiply_fusion
  (52 shorter events, 7.8 us)
Async XLA Ops:
  7.2 70.3 %all-reduce.4.cloned.1.call-start = ((), (), s32[]{:S(2)}) async-start(), calls=%async_computation | async-start | bytes 3407872 | tf_op jit(solution)/shard_map/psum | solution.py:27
  22.7 449.5 %all-reduce.6.cloned.1.call-start = ((), (), s32[]{:S(2)}) async-start(), calls=%async_computation.1 | async-start | bytes 8388608 | tf_op jit(solution)/shard_map/psum | solution.py:37
  83.0 2.7 collective-permute-start
  86.0 25.3 %collective-permute-start.1 = (f32[512,512]{0,1:T(8,128)S(1)}, f32[512,512]{0,1:T(8,128)S(1)}, u32[]{:S(2)}, u32[]{:S(2)}) collective-permute-start(f32[512,512]{0,1:T(8,128)S(1)} %add.71), channel_id=1, source_target_pairs={{0,8},{4,12},{8,0},{12,4},{16,24},{20,28},{24,16},{28,20},{32,40},... | collective-permute-start | bytes 3145736 | tf_op jit(solution)/shard_map/ppermute | solution.py:11
  111.4 26.0 %collective-permute-start.2 = (f32[512,512]{0,1:T(8,128)S(1)}, f32[512,512]{0,1:T(8,128)S(1)}, u32[]{:S(2)}, u32[]{:S(2)}) collective-permute-start(f32[512,512]{0,1:T(8,128)S(1)} %add.72), channel_id=1, source_target_pairs={{0,16},{4,20},{8,24},{12,28},{16,0},{20,4},{24,8},{28,12},{32,48},... | collective-permute-start | bytes 3145736 | tf_op jit(solution)/shard_map/ppermute | solution.py:11
  137.6 23.6 %collective-permute-start.3 = (f32[512,512]{0,1:T(8,128)S(1)}, f32[512,512]{0,1:T(8,128)S(1)}, u32[]{:S(2)}, u32[]{:S(2)}) collective-permute-start(f32[512,512]{0,1:T(8,128)S(1)} %add.73), channel_id=1, source_target_pairs={{0,32},{4,36},{8,40},{12,44},{16,48},{20,52},{24,56},{28,60},{32,0... | collective-permute-start | bytes 3145736 | tf_op jit(solution)/shard_map/ppermute | solution.py:11
  161.4 24.3 %collective-permute-start.4 = (f32[512,512]{0,1:T(8,128)S(1)}, f32[512,512]{0,1:T(8,128)S(1)}, u32[]{:S(2)}, u32[]{:S(2)}) collective-permute-start(f32[512,512]{0,1:T(8,128)S(1)} %add.74), channel_id=1, source_target_pairs={{0,64},{4,68},{8,72},{12,76},{16,80},{20,84},{24,88},{28,92},{32,9... | collective-permute-start | bytes 3145736 | tf_op jit(solution)/shard_map/ppermute | solution.py:11
  186.4 46.4 %copy-start.5 = (f32[512,512]{1,0:T(8,128)}, f32[512,512]{1,0:T(8,128)S(1)}, u32[]{:S(2)}) copy-start(f32[512,512]{1,0:T(8,128)S(1)} %fusion.10) | copy-start | bytes 3145732
  233.7 110.8 %slice-start = ((s8[6815744]{0:T(1024)(128)(4,1)}), s8[2621440]{0:T(1024)(128)(4,1)S(1)}, s32[]{:S(2)}) async-start(s8[6815744]{0:T(1024)(128)(4,1)} %bitcast.55), calls=%async_computation.2 | async-start | bytes 5242880
  333.6 6.8 %copy-start.4 = (f32[832,512]{1,0:T(8,128)S(1)}, f32[832,512]{1,0:T(8,128)}, u32[]{:S(2)}) copy-start(f32[832,512]{1,0:T(8,128)} %all-reduce.4.cloned.1.call-done) | copy-start | bytes 5111812
  335.9 8.6 %slice-start.1 = ((s8[6815744]{0:T(1024)(128)(4,1)}), s8[4194304]{0:T(1024)(128)(4,1)S(1)}, s32[]{:S(2)}) async-start(s8[6815744]{0:T(1024)(128)(4,1)} %bitcast.55), calls=%async_computation.3 | async-start | bytes 8388608
  336.0 8.6 %copy-start.1 = (bf16[832,2048]{1,0:T(8,128)(2,1)S(1)}, bf16[832,2048]{1,0:T(8,128)(2,1)}, u32[]{:S(2)}) copy-start(bf16[832,2048]{1,0:T(8,128)(2,1)} %param.3) | copy-start | bytes 10223620
  343.3 1.2 copy-start.3
  359.6 125.8 %copy-start.2 = (bf16[832,2048]{1,0:T(8,128)(2,1)S(1)}, bf16[832,2048]{1,0:T(8,128)(2,1)}, u32[]{:S(2)}) copy-start(bf16[832,2048]{1,0:T(8,128)(2,1)} %param.3) | copy-start | bytes 10223620
  485.5 16.5 %copy-start = (f32[2048,512]{1,0:T(8,128)S(1)}, f32[2048,512]{1,0:T(8,128)}, u32[]{:S(2)}) copy-start(f32[2048,512]{1,0:T(8,128)} %all-reduce.6.cloned.1.call-done) | copy-start | bytes 12582916
Sparse Core Ops, SparseCore 0:
  22.8 54.6 all-reduce.3
  359.8 112.4 all-reduce.5
where the time goes:
time: 520 us; the launch traced here: 512 us
  waiting for transfers between devices  260 us (50%)
  other arithmetic  131 us (25%)
  matrix products  68.2 us (13%)
  between operations  17 us (3%)
  local copies, waits for them, and re-layouts  16.8 us (3%)
  blocking collectives  10.7 us (2%)
  starting transfers between devices  7.63 us (1%)
    psum x1, waiting for transfers between devices, body(): summed = lax.psum(exact_dot(blended, left_basis, ((0,), (0,))), 'rows')  113 us
    ppermute x5, waiting for transfers between devices, partner(): lax.ppermute(shard, axis, [(i, i ^ 1 << apart) for i in range(lax.axis_si...  93.1 us
    another operation x14, other arithmetic, body(): lower_factor = jnp.linalg.cholesky(gram_whole)  80.9 us
    dot_general x5, matrix products, exact_dot(): lax.dot_general(left_arr, right_arr, (dims, ((), ())), precision=lax.Prec...  55.4 us
    psum x1, waiting for transfers between devices, body(): part_rows = lax.psum(exact_dot(blended, right_factor, ((1,), (0,))), 'cols')  54.7 us
    another operation x3, other arithmetic, body(): lax.linalg.triangular_solve(lower_factor, jnp.eye(rank_width, dtype=lower...  42.5 us
    another operation x12, local copies, waits for them, and re-layouts  14.1 us
    psum x1, blocking collectives, body(): col_squares = lax.psum(jnp.sum(summed * summed, axis=0), 'cols')  10.7 us
  transfers between devices with their start and end apart: 7, of which 7 were waited for; matrix products, arithmetic and copies ran while one was open for 0% of the time, Pallas kernels for 0%

commit v1 on v0

v1 whole, which is shorter than its diff:
```python
import jax
import jax.numpy as jnp
from jax import lax
from jax.experimental import pallas as pl
from jax.experimental.pallas import tpu as pltpu
from jax.sharding import PartitionSpec as P

momentum_decay = 0.95
norm_eps = 1e-06

F32 = jnp.float32
BF = jnp.bfloat16
M = 832
N = 2048
R = 512
YC = 208
BK = 128
NB = R // BK
TRI = [(i, j) for i in range(NB) for j in range(i, NB)]
GH = len(TRI) * BK // 2
GP = GH // 16
N_SEMS = 112


def split2(x):
    h = x.astype(BF)
    return h, (x - h.astype(F32)).astype(BF)


def split3(x):
    h = x.astype(BF)
    r = x - h.astype(F32)
    m = r.astype(BF)
    return h, m, (r - m.astype(F32)).astype(BF)


def dot(a, b, ca=1, cb=0):
    return lax.dot_general(a, b, (((ca,), (cb,)), ((), ())), preferred_element_type=F32)


def dot3(ah, al, bh, bl, ca=1, cb=0):
    return dot(ah, bh, ca, cb) + (dot(ah, bl, ca, cb) + dot(al, bh, ca, cb))


def prod6(a, b, ca, cb):
    ah, am, al = a
    bh, bm, bl = b
    lhs = jnp.concatenate([ah, ah, am, am, ah, al], axis=ca)
    rhs = jnp.concatenate([bh, bm, bh, bm, bl, bh], axis=cb)
    return dot(lhs, rhs, ca, cb)


def small_inverse(d_ref, tick, n=BK, b=16):
    row = lax.broadcasted_iota(jnp.int32, (b, n), 0)
    lane = lax.broadcasted_iota(jnp.int32, (b, n), 1)
    for s in range(n // b):
        r0 = s * b
        strip = d_ref[r0:r0 + b, :]
        cols = [jnp.broadcast_to(strip[:, r0 + j:r0 + j + 1], (b, n)) for j in range(b)]
        inside = (lane >= r0) & (lane < r0 + b)
        rows = jnp.where(inside, jnp.where(lane - r0 == row, 1.0, 0.0), strip)
        scale = jnp.zeros((b, n), F32)
        for j in range(b):
            pivot = jnp.broadcast_to(cols[j][j:j + 1], (b, n))
            scale = jnp.where(row == j, lax.rsqrt(pivot), scale)
            if j < b - 1:
                f = jnp.where(row > j, cols[j] * (1.0 / pivot), 0.0)
                for k in range(j + 1, b):
                    cols[k] = cols[k] - f * jnp.broadcast_to(cols[k][j:j + 1], (b, n))
                rows = rows - f * jnp.broadcast_to(rows[j:j + 1], (b, n))
        rows = rows * scale
        d_ref[r0:r0 + b, :] = rows
        if s < n // b - 1:
            sp = split3(rows)
            upd = prod6(sp, sp, 0, 0)
            t0 = r0 + b
            old = d_ref[t0:, :]
            lane2 = lax.broadcasted_iota(jnp.int32, old.shape, 1)
            old = jnp.where((lane2 >= r0) & (lane2 < t0), 0.0, old)
            d_ref[t0:, :] = old - upd[t0:, :]
        tick()


def chol_inverse(x_ref, d_ref, tick):
    ri = lax.broadcasted_iota(jnp.int32, (BK, BK), 0)
    ci = lax.broadcasted_iota(jnp.int32, (BK, BK), 1)
    for k in range(NB):
        k0 = k * BK
        d_ref[...] = x_ref[k0:k0 + BK, k0:k0 + BK]
        small_inverse(d_ref, tick)
        own = jnp.where(ci <= ri, d_ref[...], 0.0)
        own_split = split3(own)
        parts = []
        for j in range(NB):
            j0 = j * BK
            if j == k:
                parts.append(own)
            else:
                parts.append(prod6(own_split, split3(x_ref[k0:k0 + BK, j0:j0 + BK]), 1, 0))
            x_ref[k0:k0 + BK, j0:j0 + BK] = parts[j]
        sp = [split3(q) for q in parts]
        for i in range(k + 1, NB):
            for j in list(range(k + 1)) + list(range(i, NB)):
                u = prod6(sp[i], sp[j], 0, 0)
                i0, j0 = i * BK, j * BK
                if j == k:
                    x_ref[i0:i0 + BK, j0:j0 + BK] = -u
                else:
                    x_ref[i0:i0 + BK, j0:j0 + BK] = x_ref[i0:i0 + BK, j0:j0 + BK] - u


def mo(v, m=8):
    return pl.multiple_of(v, m)


class Copies:
    def __init__(self, send, recv):
        self.send, self.recv, self.n, self.all = send, recv, 0, []

    def start(self, src, dst, dev):
        i = self.n
        self.n += 1
        assert i < N_SEMS
        c = pltpu.make_async_remote_copy(
            src_ref=src, dst_ref=dst, send_sem=self.send.at[i], recv_sem=self.recv.at[i],
            device_id=dev, device_id_type=pl.DeviceIdType.MESH)
        c.start()
        self.all.append(c)
        return c

    def finish(self):
        for c in self.all:
            c.wait_send()


def add_into(dst, *srcs):
    t = dst[...]
    for s in srcs:
        t = t + s[...]
    dst[...] = t


class RingSum:
    def __init__(self, cp, half, buf, first, second, up, dn, a):
        self.cp, self.half, self.buf, self.up, self.dn = cp, half, buf, up, dn
        self.first, self.second = first, second
        self.me, self.u, self.d, self.o = a, lax.rem(a + 1, 4), lax.rem(a + 3, 4), lax.rem(a + 2, 4)

    def far(self):
        self.c1 = self.cp.start(self.half(self.buf, self.o, 0), self.first[0], self.up)
        self.c2 = self.cp.start(self.half(self.buf, self.o, 1), self.first[1], self.dn)

    def near_up(self):
        self.c3 = self.cp.start(self.half(self.buf, self.u, 1), self.half(self.second[0], 0, 1), self.up)

    def near_dn(self):
        self.c4 = self.cp.start(self.half(self.buf, self.d, 0), self.half(self.second[1], 0, 0), self.dn)

    def pass_up(self):
        self.c1.wait_recv()
        add_into(self.half(self.buf, self.u, 0), self.first[0])
        self.c5 = self.cp.start(self.half(self.buf, self.u, 0), self.half(self.second[0], 0, 0), self.up)

    def pass_dn(self):
        self.c2.wait_recv()
        add_into(self.half(self.buf, self.d, 1), self.first[1])
        self.c6 = self.cp.start(self.half(self.buf, self.d, 1), self.half(self.second[1], 0, 1), self.dn)

    def end(self, dst):
        self.c4.wait_recv()
        self.c5.wait_recv()
        self.c3.wait_recv()
        self.c6.wait_recv()
        for h in (0, 1):
            dst(h)[...] = (self.half(self.buf, self.me, h)[...] + self.half(self.second[0], 0, h)[...]) + self.half(self.second[1], 0, h)[...]


class RingGather:
    def __init__(self, cp, whole, half, buf, up, dn, a):
        self.cp, self.whole, self.half, self.buf, self.up, self.dn = cp, whole, half, buf, up, dn
        self.me, self.u, self.d = a, lax.rem(a + 1, 4), lax.rem(a + 3, 4)

    def start(self):
        w = self.whole(self.buf, self.me)
        self.c1 = self.cp.start(w, w, self.up)
        self.c2 = self.cp.start(w, w, self.dn)

    def forward(self):
        self.c1.wait_recv()
        h = self.half(self.buf, self.d, 0)
        self.c3 = self.cp.start(h, h, self.up)
        self.c2.wait_recv()
        h = self.half(self.buf, self.u, 1)
        self.c4 = self.cp.start(h, h, self.dn)

    def end(self):
        self.c3.wait_recv()
        self.c4.wait_recv()


def y_half(ref, c, h):
    return ref.at[pl.ds(mo(c * YC + h * (YC // 2)), YC // 2), :]


def y_whole(ref, c):
    return ref.at[pl.ds(mo(c * YC), YC), :]


def t1_half(ref, c, h):
    return ref.at[pl.ds(mo(c * 32 + h * 16), 16), :]


def t1_whole(ref, c):
    return ref.at[pl.ds(mo(c * 32), 32), :]


def t2_half(ref, c, h):
    return ref.at[pl.ds(mo(c * 8), 8), pl.ds(h * (N // 2), N // 2)]


def t2_whole(ref, c):
    return ref.at[pl.ds(mo(c * 8), 8), :]


def big_kernel(mom_hbm, grad_hbm, rf_hbm, st_ref, q_ref, scale_ref,
               mom, grad, rf, bh, bl, rfh, rfl, part, left, lth, ltl,
               y1u, y1d, y2u, y2d,
               gloc, gx, gsl, gmine, gys, gall, x_ref, d_ref,
               tt, tin, tacc, t1a, t1b, t2a, t2b, tmid, u1a, u1b, u2a, u2b, tall,
               sq_mine, sq_in, send, recv, load):
    rows, y = lax.axis_index("rows"), lax.axis_index("cols")
    core = lax.rem(rows, 2)
    chip = rows // 2
    z, x = lax.rem(chip, 4), chip // 4

    def dev(x_, z_, c_, y_):
        return ((x_ * 4 + z_) * 2 + c_, y_)

    def nxt(v, d):
        return lax.rem(v + d, 4)

    y_peer = {d: dev(x, z, core, nxt(y, d)) for d in (1, 2, 3)}
    x_peer = {d: dev(nxt(x, d), z, core, y) for d in (1, 2, 3)}
    z_peer = {d: dev(x, nxt(z, d), core, y) for d in (1, 2, 3)}
    sib = dev(x, z, 1 - core, y)
    plane = {d: (lax.rem(chip + d, 16) * 2 + core, y) for d in range(1, 16)}

    O, U, D = nxt(y, 2), nxt(y, 1), nxt(y, 3)
    order = [O, U, D, y]
    loads = [pltpu.make_async_copy(rf_hbm, rf, load.at[0])]
    for n, c in enumerate(order):
        loads.append(pltpu.make_async_copy(y_whole(mom_hbm, c), y_whole(mom, c), load.at[1 + 2 * n]))
        loads.append(pltpu.make_async_copy(y_whole(grad_hbm, c), y_whole(grad, c), load.at[2 + 2 * n]))
    for c in loads:
        c.start()

    barrier = pltpu.get_barrier_semaphore()
    peers = list(y_peer.values()) + list(plane.values()) + [sib]
    for p in peers:
        pl.semaphore_signal(barrier, inc=1, device_id=p, device_id_type=pl.DeviceIdType.MESH)

    cp = Copies(send, recv)
    loads[0].wait()
    h, l = split2(rf[...])
    rfh[...] = h
    rfl[...] = l

    def left_part(n):
        loads[1 + 2 * n].wait()
        loads[2 + 2 * n].wait()
        s = pl.ds(mo(order[n] * YC, 16), YC)
        h, l = split2(mom[s, :] + grad[s, :].astype(F32))
        bh[s, :] = h
        bl[s, :] = l
        part[s, :] = dot3(h, l, rfh[...], rfl[...])

    ring = RingSum(cp, y_half, part, (y1u, y1d), (y2u, y2d), y_peer[1], y_peer[3], y)
    left_part(0)
    pl.semaphore_wait(barrier, len(peers))
    ring.far()
    left_part(1)
    ring.near_up()
    left_part(2)
    ring.near_dn()
    left_part(3)
    ring.pass_up()
    ring.pass_dn()
    ring.end(lambda h: y_half(left, y, h))
    gather = RingGather(cp, y_whole, y_half, left, y_peer[1], y_peer[3], y)
    gather.start()

    sp = split3(y_whole(left, y)[...])
    for b, (i, j) in enumerate(TRI):
        g = prod6([s[:, i * BK:(i + 1) * BK] for s in sp], [s[:, j * BK:(j + 1) * BK] for s in sp], 0, 0)
        gloc[b * BK:(b + 1) * BK, :] = g
    c_core = cp.start(gloc.at[pl.ds(mo((1 - core) * GH), GH), :], gx, sib)

    def t_part(n, first=False):
        c = order[n]
        lt = jnp.transpose(y_whole(left, c)[...])
        h, l = split2(lt)
        lth[...] = h
        ltl[...] = l
        s = pl.ds(mo(c * YC, 16), YC)

        @pl.loop(0, N // 256)
        def _(n_):
            k = pl.ds(mo(n_ * 256, 256), 256)
            v = dot3(lth[...], ltl[...], bh[s, k], bl[s, k])
            if first:
                tt[:, k] = v
            else:
                tt[:, k] = tt[:, k] + v

    t_part(3, True)
    c_core.wait_recv()
    gh = pl.ds(mo(core * GH), GH)
    gx[...] = gx[...] + gloc[gh, :]

    def piece(ref, c):
        return ref.at[pl.ds(mo(c * GP), GP), :]

    cs = [cp.start(piece(gx, lax.rem(chip + d, 16)), gsl.at[d], plane[d]) for d in range(1, 16)]
    for c in cs:
        c.wait_recv()
    t = piece(gx, chip)[...]
    for d in range(1, 16):
        t = t + gsl[d]
    gmine[...] = t
    gys[y] = t
    cs = [cp.start(gmine, gys.at[y], y_peer[d]) for d in (1, 2, 3)]
    for c in cs:
        c.wait_recv()
    mine = piece(gall, core * 16 + chip)
    mine[...] = (gys[0] + gys[1]) + (gys[2] + gys[3])
    cs = [cp.start(mine, mine, plane[d]) for d in range(1, 16)]
    gather.forward()
    t_part(1)
    t_part(2)
    for c in cs:
        c.wait_recv()
    half = gall.at[gh, :]
    c_core = cp.start(half, half, sib)
    gather.end()
    t_part(0)
    c_core.wait_recv()
    for b, (i, j) in enumerate(TRI):
        x_ref[i * BK:(i + 1) * BK, j * BK:(j + 1) * BK] = gall[b * BK:(b + 1) * BK, :]

    def t_steps():
        up = [(x_peer[1], x_peer[3], x), (z_peer[1], z_peer[3], z)]
        c0 = []
        for p in (0, 1):
            c0.append(cp.start(tt.at[pl.ds(mo((1 - core) * 256 + p * 128), 128), :], tin.at[p], sib))
        yield
        r1 = []
        for p in (0, 1):
            c0[p].wait_recv()
            tacc[p] = tin[p] + tt[pl.ds(mo(core * 256 + p * 128), 128), :]
            r = RingSum(cp, t1_half, tacc.at[p], (t1a.at[p], t1b.at[p]), (t2a.at[p], t2b.at[p]), *up[p])
            r.far()
            r.near_up()
            r.near_dn()
            r1.append(r)
        yield
        for r in r1:
            r.pass_up()
            r.pass_dn()
        yield
        r2 = []
        for p in (0, 1):
            r1[p].end(lambda h: t1_half(tmid.at[p], 0, h))
            r = RingSum(cp, t2_half, tmid.at[p], (u1a.at[p], u1b.at[p]), (u2a.at[p], u2b.at[p]), *up[1 - p])
            r.far()
            r.near_up()
            r.near_dn()
            r2.append(r)
        yield
        for r in r2:
            r.pass_up()
            r.pass_dn()
        yield
        g2 = []
        for p in (0, 1):
            base = core * 256 + p * 128
            mid = tall.at[pl.ds(mo(base + up[p][2] * 32), 32), :]
            r2[p].end(lambda h: t2_half(mid, up[1 - p][2], h))
            g = RingGather(cp, t2_whole, t2_half, mid, *up[1 - p])
            g.start()
            g2.append(g)
        yield
        for g in g2:
            g.forward()
        yield
        g1 = []
        for p in (0, 1):
            g2[p].end()
            g = RingGather(cp, t1_whole, t1_half, tall.at[pl.ds(mo(core * 256 + p * 128), 128), :], *up[p])
            g.start()
            g1.append(g)
        yield
        for g in g1:
            g.forward()
        yield
        c1 = []
        for p in (0, 1):
            g1[p].end()
            h = tall.at[pl.ds(mo(core * 256 + p * 128), 128), :]
            c1.append(cp.start(h, h, sib))
        yield
        for c in c1:
            c.wait_recv()

    steps = t_steps()
    count = [0]
    when = {0: 0, 3: 1, 8: 2, 12: 3, 15: 4, 17: 5, 19: 6, 21: 7, 26: 8, 30: 9}

    def tick():
        if count[0] in when:
            next(steps, None)
        count[0] += 1

    tick()
    chol_inverse(x_ref, d_ref, tick)
    for _ in steps:
        pass

    vs = [split2(x_ref[i * BK:(i + 1) * BK, :(i + 1) * BK]) for i in range(NB)]

    @pl.loop(0, N // 256)
    def _(n_):
        k = pl.ds(mo(n_ * 256, 256), 256)
        th, tl = split2(tall[:, k])
        for i in range(NB):
            e = (i + 1) * BK
            v = dot3(vs[i][0], vs[i][1], th[:e], tl[:e])
            st_ref[i * BK:e, k] = v

    sq = jnp.zeros((R, 128), F32)
    for n_ in range(N // 128):
        v = st_ref[:, n_ * 128:(n_ + 1) * 128]
        sq = sq + v * v
    ones = jnp.ones((8, 128), BF)
    sh, sm, sl = split3(sq)
    sq_mine[...] = dot(ones, sh, 1, 1) + (dot(ones, sm, 1, 1) + dot(ones, sl, 1, 1))
    cs = [cp.start(sq_mine, sq_in.at[d], y_peer[d]) for d in (1, 2, 3)]
    lh, ll = split2(left[...])
    for j in range(NB):
        e = (j + 1) * BK
        q_ref[:, j * BK:e] = dot3(lh[:, :e], ll[:, :e], vs[j][0], vs[j][1], 1, 1)
    for c in cs:
        c.wait_recv()
    scale_ref[...] = lax.rsqrt(sq_mine[...] + sq_in[1] + sq_in[2] + sq_in[3] + norm_eps)
    cp.finish()


def last_kernel(mom_ref, grad_ref, q_ref, st_ref, scale_ref, nm_ref, nf_ref, lb_ref):
    @pl.when(pl.program_id(0) == 0)
    def _():
        lb_ref[...] = q_ref[...]

    st = st_ref[...]
    nm_ref[...] = (mom_ref[...] + grad_ref[...].astype(F32)) - (1.0 - momentum_decay) * dot(
        q_ref[...].astype(BF), st.astype(BF))
    nf_ref[...] = jnp.transpose(st) * scale_ref[0:1, :]


def body(gradient, momentum, right_factor):
    V = pltpu.VMEM
    big = pl.pallas_call(
        big_kernel,
        out_shape=(jax.ShapeDtypeStruct((R, N), F32), jax.ShapeDtypeStruct((M, R), F32),
                   jax.ShapeDtypeStruct((8, R), F32)),
        in_specs=[pl.BlockSpec(memory_space=pl.ANY)] * 3,
        out_specs=[pl.BlockSpec(memory_space=V)] * 3,
        scratch_shapes=[
            V((M, N), F32), V((M, N), BF), V((N, R), F32), V((M, N), BF), V((M, N), BF),
            V((N, R), BF), V((N, R), BF), V((M, R), F32), V((M, R), F32), V((R, YC), BF), V((R, YC), BF),
            V((YC // 2, R), F32), V((YC // 2, R), F32), V((YC, R), F32), V((YC, R), F32),
            V((2 * GH, BK), F32), V((GH, BK), F32), V((16, GP, BK), F32), V((GP, BK), F32), V((4, GP, BK), F32),
            V((2 * GH, BK), F32), V((R, R), F32), V((BK, BK), F32),
            V((R, N), F32), V((2, 128, N), F32), V((2, 128, N), F32),
            V((2, 16, N), F32), V((2, 16, N), F32), V((2, 32, N), F32), V((2, 32, N), F32), V((2, 32, N), F32),
            V((2, 8, N // 2), F32), V((2, 8, N // 2), F32), V((2, 8, N), F32), V((2, 8, N), F32), V((R, N), F32),
            V((8, R), F32), V((4, 8, R), F32),
            pltpu.SemaphoreType.DMA((N_SEMS,)), pltpu.SemaphoreType.DMA((N_SEMS,)), pltpu.SemaphoreType.DMA((9,)),
        ],
        compiler_params=pltpu.CompilerParams(
            collective_id=0, has_side_effects=True, vmem_limit_bytes=60 << 20),
        cost_estimate=pl.CostEstimate(flops=4 * M * N * R * 3, bytes_accessed=20 << 20, transcendentals=0),
    )
    st, q, scale = big(momentum, gradient, right_factor)
    tile = 256
    return pl.pallas_call(
        last_kernel,
        grid=(N // tile,),
        out_shape=(jax.ShapeDtypeStruct((M, N), F32), jax.ShapeDtypeStruct((N, R), F32),
                   jax.ShapeDtypeStruct((M, R), F32)),
        in_specs=[pl.BlockSpec((M, tile), lambda n: (0, n)), pl.BlockSpec((M, tile), lambda n: (0, n)),
                  pl.BlockSpec((M, R), lambda n: (0, 0)), pl.BlockSpec((R, tile), lambda n: (0, n)),
                  pl.BlockSpec((8, R), lambda n: (0, 0))],
        out_specs=[pl.BlockSpec((M, tile), lambda n: (0, n)), pl.BlockSpec((tile, R), lambda n: (n, 0)),
                   pl.BlockSpec((M, R), lambda n: (0, 0))],
        compiler_params=pltpu.CompilerParams(vmem_limit_bytes=40 << 20),
        cost_estimate=pl.CostEstimate(flops=2 * M * N * R, bytes_accessed=30 << 20, transcendentals=0),
    )(momentum, gradient, q, st, scale)


def solution(mesh):
    return jax.shard_map(
        body,
        mesh=mesh,
        in_specs=(P("rows", "cols"), P("rows", "cols"), P("cols", None)),
        out_specs=(P("rows", "cols"), P("cols", None), P("rows", None)),
        check_vma=False,
    )
```

time: 520 us -> 131 us (0.25); the launches traced: 512 us -> 129 us
  waiting for transfers between devices: 260 us -> 0 us
  other arithmetic: 131 us -> 0 us
  Pallas kernels: 0 us -> 124 us
  matrix products: 68.2 us -> 0 us
  between operations: 17 us -> 0.66 us
  local copies, waits for them, and re-layouts: 16.8 us -> 4.36 us
  blocking collectives: 10.7 us -> 0 us
  starting transfers between devices: 7.63 us -> 0 us
    psum x2 -> x0, waiting for transfers between devices: 167 us -> none  [the longest x1 113 us: body(): summed = lax.psum(exact_dot(blended, left_basis, ((0,), (0,))), 'rows')]
    pallas_call x0 -> x2, Pallas kernels: none -> 124 us  [the longest x1 113 us: body(): st, q, scale = big(momentum, gradient, right_factor)]
    another operation x17 -> x0, other arithmetic: 123 us -> none  [the longest x14 80.9 us: body(): lower_factor = jnp.linalg.cholesky(gram_whole)]
    ppermute x5 -> x0, waiting for transfers between devices: 93.1 us -> none  [partner(): lax.ppermute(shard, axis, [(i, i ^ 1 << apart) for i in range(lax.axis_si...]
    dot_general x5 -> x0, matrix products: 55.4 us -> none  [exact_dot(): lax.dot_general(left_arr, right_arr, (dims, ((), ())), precision=lax.Prec...]
    another operation x17 -> x0, local copies, waits for them, and re-layouts: 15.2 us -> none
    another operation x13 -> x0, matrix products: 12.7 us -> none  [the longest x7 6.69 us: body(): lax.linalg.triangular_solve(lower_factor, jnp.eye(rank_width, dtype=lower...]
    psum x1 -> x0, blocking collectives: 10.7 us -> none  [body(): col_squares = lax.psum(jnp.sum(summed * summed, axis=0), 'cols')]
  transfers between devices with their start and end apart: 7 -> 0, of which waited for: 7 -> 0; matrix products, arithmetic and copies ran while one was open for 0% -> 0% of each run, Pallas kernels for 0% -> 0%
where the time goes in v1:
time: 131 us; the launch traced here: 129 us
  Pallas kernels  124 us (95%)
  local copies, waits for them, and re-layouts  4.36 us (3%)
    pallas_call x1, Pallas kernels, body(): st, q, scale = big(momentum, gradient, right_factor)  113 us
    pallas_call x1, Pallas kernels, body(): pl.pallas_call(last_kernel, grid=(N // tile,), out_shape=(jax.ShapeDtypeS...  10.5 us
    unnamed x8, local copies, waits for them, and re-layouts  4.36 us

profile of v1, /device:TPU:6, one launch (start us, length us, event | category | flops | bytes accessed | tf_op | source)
XLA Modules:
  0.0 129.0 jit_solution(10787433096997222563)
XLA Ops:
  0.6 0.0 copy-start.1
  0.6 113.4 %shard_map.58 = (f32[512,2048]{1,0:T(8,128)}, f32[832,512]{1,0:T(8,128)}, f32[8,512]{1,0:T(8,128)}) custom-call(f32[832,2048]{1,0:T(8,128)} %mom_ref.1, bf16[832,2048]{1,0:T(8,128)(2,1)} %grad_ref.1, f32[2048,512]{1,0:T(8,128)} %rf_hbm.1), custom_call_target="tpu_custom_call" | custom-call | flops 10468982784 | bytes 20971520 | tf_op jit(solution)/shard_map/pallas_call | solution.py:492
  114.1 0.0 copy-done.1
  114.1 0.0 copy-start
  114.1 2.2 %copy-done = f32[512,2048]{1,0:T(8,128)S(1)} copy-done((f32[512,2048]{1,0:T(8,128)S(1)}, f32[512,2048]{1,0:T(8,128)}, u32[]{:S(2)}) %copy-start) | copy-done | bytes 4194328
  116.3 0.0 copy-start.2
  116.3 1.5 %copy-done.2 = f32[832,512]{1,0:T(8,128)S(1)} copy-done((f32[832,512]{1,0:T(8,128)S(1)}, f32[832,512]{1,0:T(8,128)}, u32[]{:S(2)}) %copy-start.2) | copy-done | bytes 1703960
  117.7 0.0 copy-start.3
  117.7 0.7 copy-done.3
  118.4 10.5 %shard_map.59 = (f32[832,2048]{1,0:T(8,128)}, f32[2048,512]{1,0:T(8,128)}, f32[832,512]{1,0:T(8,128)}) custom-call(f32[832,2048]{1,0:T(8,128)} %mom_ref.1, bf16[832,2048]{1,0:T(8,128)(2,1)S(1)} %copy-done.1, f32[832,512]{1,0:T(8,128)S(1)} %copy-done.2, f32[512,2048]{1,0:T(8,128)S(1)} %copy-done, f32[8,512]{1,0:T(8,128)S(1)} %copy-done.3), custom_call_target="tpu_custom_call" | custom-call | flops 1744830464 | bytes 31457280 | tf_op jit(solution)/shard_map/pallas_call | solution.py:494
Async XLA Ops:
  0.6 113.4 %copy-start.1 = (bf16[832,2048]{1,0:T(8,128)(2,1)S(1)}, bf16[832,2048]{1,0:T(8,128)(2,1)}, u32[]{:S(2)}) copy-start(bf16[832,2048]{1,0:T(8,128)(2,1)} %grad_ref.1) | copy-start | bytes 10223620
  114.1 2.2 %copy-start = (f32[512,2048]{1,0:T(8,128)S(1)}, f32[512,2048]{1,0:T(8,128)}, u32[]{:S(2)}) copy-start(f32[512,2048]{1,0:T(8,128)} %get-tuple-element.7.st_ref) | copy-start | bytes 12582916
  116.3 1.5 %copy-start.2 = (f32[832,512]{1,0:T(8,128)S(1)}, f32[832,512]{1,0:T(8,128)}, u32[]{:S(2)}) copy-start(f32[832,512]{1,0:T(8,128)} %get-tuple-element.6.q_ref) | copy-start | bytes 5111812
  117.7 0.7 copy-start.3

commit v2 on v1

--- a/solution.py
+++ b/solution.py
@@ -19,7 +19,7 @@
 TRI = [(i, j) for i in range(NB) for j in range(i, NB)]
 GH = len(TRI) * BK // 2
 GP = GH // 16
-N_SEMS = 112
+N_SEMS = 220
 
 
 def split2(x):
@@ -131,6 +131,7 @@
     def finish(self):
         for c in self.all:
             c.wait_send()
+        self.all = []
 
 
 def add_into(dst, *srcs):
@@ -206,28 +207,103 @@
     return ref.at[pl.ds(mo(c * YC), YC), :]
 
 
-def t1_half(ref, c, h):
-    return ref.at[pl.ds(mo(c * 32 + h * 16), 16), :]
-
-
-def t1_whole(ref, c):
-    return ref.at[pl.ds(mo(c * 32), 32), :]
-
-
-def t2_half(ref, c, h):
+def t_half(ref, c, h):
     return ref.at[pl.ds(mo(c * 8), 8), pl.ds(h * (N // 2), N // 2)]
 
 
-def t2_whole(ref, c):
+def t_whole(ref, c):
     return ref.at[pl.ds(mo(c * 8), 8), :]
 
 
-def big_kernel(mom_hbm, grad_hbm, rf_hbm, st_ref, q_ref, scale_ref,
-               mom, grad, rf, bh, bl, rfh, rfl, part, left, lth, ltl,
+def t_quarter(ref, c):
+    return ref.at[:, pl.ds(mo(c * (N // 4), 128), N // 4)]
+
+
+class GroupSum:
+    def __init__(self, cp, g, core, ups, tt, tin, r1, r2, tmid, rq, tall, sib):
+        self.cp, self.g, self.core, self.ups, self.sib = cp, g, core, ups, sib
+        self.tt, self.tin, self.r1, self.r2, self.tmid, self.rq = tt, tin, r1, r2, tmid, rq
+        self.tall = tall
+
+    def pair(self):
+        src = self.tt.at[pl.ds(mo(self.g * BK + (1 - self.core) * 64), 64), :]
+        self.c0 = self.cp.start(src, self.tin.at[self.g], self.sib)
+
+    def ring(self):
+        self.c0.wait_recv()
+        g = self.g
+        own = self.tt.at[pl.ds(mo(g * BK + self.core * 64), 64), :]
+        own[...] = self.tin[g] + own[...]
+        self.rings = []
+        for p in (0, 1):
+            peer, a = self.ups[p]
+            r = RingSum(self.cp, t_half, self.tt.at[pl.ds(mo(g * BK + self.core * 64 + 32 * p), 32), :],
+                        (self.r1.at[g, p, 0], self.r1.at[g, p, 1]), (self.r2.at[g, p, 0], self.r2.at[g, p, 1]),
+                        peer[1], peer[3], a)
+            r.far()
+            r.near_up()
+            r.near_dn()
+            self.rings.append(r)
+
+    def ring_pass(self):
+        for r in self.rings:
+            r.pass_up()
+            r.pass_dn()
+
+    def direct(self):
+        self.cq = []
+        for p in (0, 1):
+            mid = self.tmid.at[self.g, p]
+            self.rings[p].end(lambda h: t_half(mid, 0, h))
+            peer, a = self.ups[1 - p]
+            for d in (1, 2, 3):
+                self.cq.append(self.cp.start(t_quarter(mid, lax.rem(a + d, 4)), self.rq.at[self.g, p, d], peer[d]))
+
+    def base(self, p):
+        return self.tall.at[pl.ds(mo(self.g * BK + self.core * 64 + 32 * p), 32), :]
+
+    def spread(self):
+        for c in self.cq:
+            c.wait_recv()
+        self.cq = []
+        for p in (0, 1):
+            peer, a = self.ups[1 - p]
+            rq = self.rq.at[self.g, p]
+            out = t_quarter(t_whole(self.base(p), self.ups[p][1]), a)
+            out[...] = (t_quarter(self.tmid.at[self.g, p], a)[...] + rq[1]) + (rq[2] + rq[3])
+            for d in (1, 2, 3):
+                self.cq.append(self.cp.start(out, out, peer[d]))
+
+    def gather(self):
+        for c in self.cq:
+            c.wait_recv()
+        self.gathers = []
+        for p in (0, 1):
+            peer, a = self.ups[p]
+            r = RingGather(self.cp, t_whole, t_half, self.base(p), peer[1], peer[3], a)
+            r.start()
+            self.gathers.append(r)
+
+    def gather_pass(self):
+        for r in self.gathers:
+            r.forward()
+
+    def share(self):
+        for r in self.gathers:
+            r.end()
+        h = self.tall.at[pl.ds(mo(self.g * BK + self.core * 64), 64), :]
+        self.c1 = self.cp.start(h, h, self.sib)
+
+    def done(self):
+        self.c1.wait_recv()
+
+
+def big_kernel(mom_hbm, grad_hbm, rf_hbm, st_hbm, q_hbm, scale_ref,
+               mom, rf, bh, bl, rfh, rfl, part, left, ltc,
                y1u, y1d, y2u, y2d,
                gloc, gx, gsl, gmine, gys, gall, x_ref, d_ref,
-               tt, tin, tacc, t1a, t1b, t2a, t2b, tmid, u1a, u1b, u2a, u2b, tall,
-               sq_mine, sq_in, send, recv, load):
+               tin, r1, r2, tmid, rq, tall, st,
+               sq_mine, sq_in, send, recv, load, rounds):
     rows, y = lax.axis_index("rows"), lax.axis_index("cols")
     core = lax.rem(rows, 2)
     chip = rows // 2
@@ -250,14 +326,18 @@
     loads = [pltpu.make_async_copy(rf_hbm, rf, load.at[0])]
     for n, c in enumerate(order):
         loads.append(pltpu.make_async_copy(y_whole(mom_hbm, c), y_whole(mom, c), load.at[1 + 2 * n]))
-        loads.append(pltpu.make_async_copy(y_whole(grad_hbm, c), y_whole(grad, c), load.at[2 + 2 * n]))
+        loads.append(pltpu.make_async_copy(y_whole(grad_hbm, c), y_whole(bh, c), load.at[2 + 2 * n]))
     for c in loads:
         c.start()
 
     barrier = pltpu.get_barrier_semaphore()
-    peers = list(y_peer.values()) + list(plane.values()) + [sib]
-    for p in peers:
-        pl.semaphore_signal(barrier, inc=1, device_id=p, device_id_type=pl.DeviceIdType.MESH)
+    near = [p[d] for p in (x_peer, y_peer, z_peer) for d in (1, 3)] + [sib]
+
+    def greet(sem):
+        for p in near:
+            pl.semaphore_signal(sem, inc=1, device_id=p, device_id_type=pl.DeviceIdType.MESH)
+
+    greet(barrier)
 
     cp = Copies(send, recv)
     loads[0].wait()
@@ -269,50 +349,64 @@
         loads[1 + 2 * n].wait()
         loads[2 + 2 * n].wait()
         s = pl.ds(mo(order[n] * YC, 16), YC)
-        h, l = split2(mom[s, :] + grad[s, :].astype(F32))
+        h, l = split2(mom[s, :] + bh[s, :].astype(F32))
         bh[s, :] = h
         bl[s, :] = l
-        part[s, :] = dot3(h, l, rfh[...], rfl[...])
-
-    ring = RingSum(cp, y_half, part, (y1u, y1d), (y2u, y2d), y_peer[1], y_peer[3], y)
+        v = dot3(h, l, rfh[...], rfl[...])
+        for g in range(NB):
+            part[g, s, :] = v[:, g * BK:(g + 1) * BK]
+
+    rings = [RingSum(cp, y_half, part.at[g], (y1u.at[g], y1d.at[g]), (y2u.at[g], y2d.at[g]), y_peer[1], y_peer[3], y)
+             for g in range(NB)]
+    gathers = [RingGather(cp, y_whole, y_half, left.at[g], y_peer[1], y_peer[3], y) for g in range(NB)]
     left_part(0)
-    pl.semaphore_wait(barrier, len(peers))
-    ring.far()
+    pl.semaphore_wait(barrier, len(near))
+    for r in rings:
+        r.far()
+    greet(rounds.at[0])
     left_part(1)
-    ring.near_up()
+    for r in rings:
+        r.near_up()
     left_part(2)
-    ring.near_dn()
+    for r in rings:
+        r.near_dn()
     left_part(3)
-    ring.pass_up()
-    ring.pass_dn()
-    ring.end(lambda h: y_half(left, y, h))
-    gather = RingGather(cp, y_whole, y_half, left, y_peer[1], y_peer[3], y)
-    gather.start()
-
-    sp = split3(y_whole(left, y)[...])
+    pl.semaphore_wait(rounds.at[0], len(near))
+    greet(rounds.at[1])
+    for r in rings:
+        r.pass_up()
+        r.pass_dn()
+    pl.semaphore_wait(rounds.at[1], len(near))
+    greet(rounds.at[2])
+    own = pl.ds(mo(y * YC), YC)
+    for g in range(NB):
+        rings[g].end(lambda h: y_half(left.at[g], y, h))
+        if g < 2:
+            gathers[g].start()
+
+    sp = [split3(left[g, own, :]) for g in range(NB)]
     for b, (i, j) in enumerate(TRI):
-        g = prod6([s[:, i * BK:(i + 1) * BK] for s in sp], [s[:, j * BK:(j + 1) * BK] for s in sp], 0, 0)
-        gloc[b * BK:(b + 1) * BK, :] = g
+        gloc[b * BK:(b + 1) * BK, :] = prod6(sp[i], sp[j], 0, 0)
     c_core = cp.start(gloc.at[pl.ds(mo((1 - core) * GH), GH), :], gx, sib)
 
-    def t_part(n, first=False):
-        c = order[n]
-        lt = jnp.transpose(y_whole(left, c)[...])
-        h, l = split2(lt)
-        lth[...] = h
-        ltl[...] = l
-        s = pl.ds(mo(c * YC, 16), YC)
+    tt = mom
+    ups = [(x_peer, x), (z_peer, z)]
+    sums = [GroupSum(cp, g, core, ups, tt, tin, r1, r2, tmid, rq, tall, sib) for g in range(NB)]
+
+    def t_part(g):
+        gathers[g].end()
+        h, l = split2(jnp.transpose(left[g]))
+        ltc[0:BK, :] = h
+        ltc[BK:2 * BK, :] = l
 
         @pl.loop(0, N // 256)
         def _(n_):
             k = pl.ds(mo(n_ * 256, 256), 256)
-            v = dot3(lth[...], ltl[...], bh[s, k], bl[s, k])
-            if first:
-                tt[:, k] = v
-            else:
-                tt[:, k] = tt[:, k] + v
-
-    t_part(3, True)
+            v = dot(ltc[...], bh[:, k])
+            tt[g * BK:(g + 1) * BK, k] = v[:BK] + (v[BK:] + dot(ltc[0:BK, :], bl[:, k]))
+
+        sums[g].pair()
+
     c_core.wait_recv()
     gh = pl.ds(mo(core * GH), GH)
     gx[...] = gx[...] + gloc[gh, :]
@@ -320,7 +414,13 @@
     def piece(ref, c):
         return ref.at[pl.ds(mo(c * GP), GP), :]
 
+    pl.semaphore_wait(rounds.at[2], len(near))
     cs = [cp.start(piece(gx, lax.rem(chip + d, 16)), gsl.at[d], plane[d]) for d in range(1, 16)]
+    gathers[0].forward()
+    gathers[2].start()
+    gathers[1].forward()
+    gathers[3].start()
+    t_part(0)
     for c in cs:
         c.wait_recv()
     t = piece(gx, chip)[...]
@@ -329,125 +429,89 @@
     gmine[...] = t
     gys[y] = t
     cs = [cp.start(gmine, gys.at[y], y_peer[d]) for d in (1, 2, 3)]
+    gathers[2].forward()
+    sums[0].ring()
+    t_part(1)
     for c in cs:
         c.wait_recv()
     mine = piece(gall, core * 16 + chip)
     mine[...] = (gys[0] + gys[1]) + (gys[2] + gys[3])
     cs = [cp.start(mine, mine, plane[d]) for d in range(1, 16)]
-    gather.forward()
-    t_part(1)
+    gathers[3].forward()
     t_part(2)
+    sums[1].ring()
+    sums[0].ring_pass()
+    t_part(3)
+    sums[2].ring()
+    sums[1].ring_pass()
     for c in cs:
         c.wait_recv()
     half = gall.at[gh, :]
     c_core = cp.start(half, half, sib)
-    gather.end()
-    t_part(0)
+    sums[3].ring()
+    sums[0].direct()
     c_core.wait_recv()
     for b, (i, j) in enumerate(TRI):
         x_ref[i * BK:(i + 1) * BK, j * BK:(j + 1) * BK] = gall[b * BK:(b + 1) * BK, :]
 
-    def t_steps():
-        up = [(x_peer[1], x_peer[3], x), (z_peer[1], z_peer[3], z)]
-        c0 = []
-        for p in (0, 1):
-            c0.append(cp.start(tt.at[pl.ds(mo((1 - core) * 256 + p * 128), 128), :], tin.at[p], sib))
-        yield
-        r1 = []
-        for p in (0, 1):
-            c0[p].wait_recv()
-            tacc[p] = tin[p] + tt[pl.ds(mo(core * 256 + p * 128), 128), :]
-            r = RingSum(cp, t1_half, tacc.at[p], (t1a.at[p], t1b.at[p]), (t2a.at[p], t2b.at[p]), *up[p])
-            r.far()
-            r.near_up()
-            r.near_dn()
-            r1.append(r)
-        yield
-        for r in r1:
-            r.pass_up()
-            r.pass_dn()
-        yield
-        r2 = []
-        for p in (0, 1):
-            r1[p].end(lambda h: t1_half(tmid.at[p], 0, h))
-            r = RingSum(cp, t2_half, tmid.at[p], (u1a.at[p], u1b.at[p]), (u2a.at[p], u2b.at[p]), *up[1 - p])
-            r.far()
-            r.near_up()
-            r.near_dn()
-            r2.append(r)
-        yield
-        for r in r2:
-            r.pass_up()
-            r.pass_dn()
-        yield
-        g2 = []
-        for p in (0, 1):
-            base = core * 256 + p * 128
-            mid = tall.at[pl.ds(mo(base + up[p][2] * 32), 32), :]
-            r2[p].end(lambda h: t2_half(mid, up[1 - p][2], h))
-            g = RingGather(cp, t2_whole, t2_half, mid, *up[1 - p])
-            g.start()
-            g2.append(g)
-        yield
-        for g in g2:
-            g.forward()
-        yield
-        g1 = []
-        for p in (0, 1):
-            g2[p].end()
-            g = RingGather(cp, t1_whole, t1_half, tall.at[pl.ds(mo(core * 256 + p * 128), 128), :], *up[p])
-            g.start()
-            g1.append(g)
-        yield
-        for g in g1:
-            g.forward()
-        yield
-        c1 = []
-        for p in (0, 1):
-            g1[p].end()
-            h = tall.at[pl.ds(mo(core * 256 + p * 128), 128), :]
-            c1.append(cp.start(h, h, sib))
-        yield
-        for c in c1:
-            c.wait_recv()
-
-    steps = t_steps()
+    s0, s1, s2, s3 = sums
+    plan = {
+        0: [s2.ring_pass, s1.direct], 2: [s0.spread], 4: [s3.ring_pass], 6: [s2.direct], 7: [s1.spread],
+        9: [s0.gather], 10: [s3.direct], 13: [s2.spread], 14: [s1.gather], 16: [s0.gather_pass], 17: [s3.spread],
+        20: [s2.gather], 21: [s1.gather_pass], 23: [s0.share], 24: [s3.gather], 26: [s2.gather_pass],
+        27: [s1.share], 28: [s0.done], 30: [s3.gather_pass], 31: [s1.done], 32: [s2.share],
+    }
     count = [0]
-    when = {0: 0, 3: 1, 8: 2, 12: 3, 15: 4, 17: 5, 19: 6, 21: 7, 26: 8, 30: 9}
 
     def tick():
-        if count[0] in when:
-            next(steps, None)
+        for f in plan.get(count[0], ()):
+            f()
         count[0] += 1
 
     tick()
     chol_inverse(x_ref, d_ref, tick)
-    for _ in steps:
-        pass
+    for n_ in range(count[0], 40):
+        tick()
 
     vs = [split2(x_ref[i * BK:(i + 1) * BK, :(i + 1) * BK]) for i in range(NB)]
-
-    @pl.loop(0, N // 256)
-    def _(n_):
-        k = pl.ds(mo(n_ * 256, 256), 256)
-        th, tl = split2(tall[:, k])
-        for i in range(NB):
-            e = (i + 1) * BK
-            v = dot3(vs[i][0], vs[i][1], th[:e], tl[:e])
-            st_ref[i * BK:e, k] = v
-
-    sq = jnp.zeros((R, 128), F32)
-    for n_ in range(N // 128):
-        v = st_ref[:, n_ * 128:(n_ + 1) * 128]
-        sq = sq + v * v
-    ones = jnp.ones((8, 128), BF)
-    sh, sm, sl = split3(sq)
-    sq_mine[...] = dot(ones, sh, 1, 1) + (dot(ones, sm, 1, 1) + dot(ones, sl, 1, 1))
-    cs = [cp.start(sq_mine, sq_in.at[d], y_peer[d]) for d in (1, 2, 3)]
-    lh, ll = split2(left[...])
+    lh, ll = split2(jnp.concatenate([left[g] for g in range(NB)], axis=1))
+    q_buf = rf.at[0:M, :]
     for j in range(NB):
         e = (j + 1) * BK
-        q_ref[:, j * BK:e] = dot3(lh[:, :e], ll[:, :e], vs[j][0], vs[j][1], 1, 1)
+        q_buf[:, j * BK:e] = dot3(lh[:, :e], ll[:, :e], vs[j][0], vs[j][1], 1, 1)
+    out_q = pltpu.make_async_copy(q_buf, q_hbm, load.at[0])
+    out_q.start()
+    ones = jnp.ones((8, BK), BF)
+    outs = []
+
+    def summed(i):
+        e = (i + 1) * BK
+        sq = jnp.zeros((BK, BK), F32)
+        for n_ in range(N // 512):
+            k = pl.ds(n_ * 512, 512)
+            th, tl = split2(tall[:e, k])
+            v = dot3(vs[i][0], vs[i][1], th, tl)
+            st[i * BK:e, k] = v
+            for m_ in range(4):
+                w = v[:, m_ * BK:(m_ + 1) * BK]
+                sq = sq + w * w
+        sh, sm, sl = split3(sq)
+        sq_mine[:, i * BK:e] = dot(ones, sh, 1, 1) + (dot(ones, sm, 1, 1) + dot(ones, sl, 1, 1))
+        c = pltpu.make_async_copy(st.at[i * BK:e, :], st_hbm.at[i * BK:e, :], load.at[1 + i])
+        c.start()
+        outs.append(c)
+
+    summed(0)
+    s3.share()
+    summed(1)
+    s2.done()
+    summed(2)
+    s3.done()
+    summed(3)
+    cs = [cp.start(sq_mine, sq_in.at[d], y_peer[d]) for d in (1, 2, 3)]
+    cp.finish()
+    for c in [out_q] + outs:
+        c.wait()
     for c in cs:
         c.wait_recv()
     scale_ref[...] = lax.rsqrt(sq_mine[...] + sq_in[1] + sq_in[2] + sq_in[3] + norm_eps)
@@ -471,22 +535,22 @@
         big_kernel,
         out_shape=(jax.ShapeDtypeStruct((R, N), F32), jax.ShapeDtypeStruct((M, R), F32),
                    jax.ShapeDtypeStruct((8, R), F32)),
-        in_specs=[pl.BlockSpec(memory_space=pl.ANY)] * 3,
-        out_specs=[pl.BlockSpec(memory_space=V)] * 3,
+        in_specs=[pl.BlockSpec(memory_space=pltpu.HBM)] * 3,
+        out_specs=[pl.BlockSpec(memory_space=pl.ANY)] * 2 + [pl.BlockSpec(memory_space=V)],
         scratch_shapes=[
-            V((M, N), F32), V((M, N), BF), V((N, R), F32), V((M, N), BF), V((M, N), BF),
-            V((N, R), BF), V((N, R), BF), V((M, R), F32), V((M, R), F32), V((R, YC), BF), V((R, YC), BF),
-            V((YC // 2, R), F32), V((YC // 2, R), F32), V((YC, R), F32), V((YC, R), F32),
+            V((M, N), F32), V((N, R), F32), V((M, N), BF), V((M, N), BF),
+            V((N, R), BF), V((N, R), BF), V((NB, M, BK), F32), V((NB, M, BK), F32), V((2 * BK, M), BF),
+            V((NB, YC // 2, BK), F32), V((NB, YC // 2, BK), F32), V((NB, YC, BK), F32), V((NB, YC, BK), F32),
             V((2 * GH, BK), F32), V((GH, BK), F32), V((16, GP, BK), F32), V((GP, BK), F32), V((4, GP, BK), F32),
             V((2 * GH, BK), F32), V((R, R), F32), V((BK, BK), F32),
-            V((R, N), F32), V((2, 128, N), F32), V((2, 128, N), F32),
-            V((2, 16, N), F32), V((2, 16, N), F32), V((2, 32, N), F32), V((2, 32, N), F32), V((2, 32, N), F32),
-            V((2, 8, N // 2), F32), V((2, 8, N // 2), F32), V((2, 8, N), F32), V((2, 8, N), F32), V((R, N), F32),
+            V((NB, 64, N), F32),
+            V((NB, 2, 2, 8, N // 2), F32), V((NB, 2, 2, 8, N), F32), V((NB, 2, 8, N), F32),
+            V((NB, 2, 4, 8, N // 4), F32), V((R, N), F32), V((R, N), F32),
             V((8, R), F32), V((4, 8, R), F32),
-            pltpu.SemaphoreType.DMA((N_SEMS,)), pltpu.SemaphoreType.DMA((N_SEMS,)), pltpu.SemaphoreType.DMA((9,)),
+            pltpu.SemaphoreType.DMA((N_SEMS,)), pltpu.SemaphoreType.DMA((N_SEMS,)), pltpu.SemaphoreType.DMA((9,)), pltpu.SemaphoreType.REGULAR((3,)),
         ],
         compiler_params=pltpu.CompilerParams(
-            collective_id=0, has_side_effects=True, vmem_limit_bytes=60 << 20),
+            collective_id=0, has_side_effects=True, vmem_limit_bytes=50 << 20),
         cost_estimate=pl.CostEstimate(flops=4 * M * N * R * 3, bytes_accessed=20 << 20, transcendentals=0),
     )
     st, q, scale = big(momentum, gradient, right_factor)
@@ -501,7 +565,7 @@
                   pl.BlockSpec((8, R), lambda n: (0, 0))],
         out_specs=[pl.BlockSpec((M, tile), lambda n: (0, n)), pl.BlockSpec((tile, R), lambda n: (n, 0)),
                    pl.BlockSpec((M, R), lambda n: (0, 0))],
-        compiler_params=pltpu.CompilerParams(vmem_limit_bytes=40 << 20),
+        compiler_params=pltpu.CompilerParams(vmem_limit_bytes=24 << 20),
         cost_estimate=pl.CostEstimate(flops=2 * M * N * R, bytes_accessed=30 << 20, transcendentals=0),
     )(momentum, gradient, q, st, scale)
 

time: 131 us -> 103 us (0.79)
  Pallas kernels: 124 us -> 98.8 us
  local copies, waits for them, and re-layouts: 4.36 us -> 2.19 us
    pallas_call x1, Pallas kernels: 113 us -> 91.1 us  [body(): st, q, scale = big(momentum, gradient, right_factor)]
    pallas_call x1, Pallas kernels: 10.5 us -> 7.66 us  [body(): pl.pallas_call(last_kernel, grid=(N // tile,), out_shape=(jax.ShapeDtypeS...]
    unnamed x8 -> x6, local copies, waits for them, and re-layouts: 4.36 us -> 2.19 us
where the time goes in v2:
time: 103 us; the launch traced here: 102 us
  Pallas kernels  98.8 us (96%)
  local copies, waits for them, and re-layouts  2.19 us (2%)
    pallas_call x1, Pallas kernels, body(): st, q, scale = big(momentum, gradient, right_factor)  91.1 us
    pallas_call x1, Pallas kernels, body(): pl.pallas_call(last_kernel, grid=(N // tile,), out_shape=(jax.ShapeDtypeS...  7.66 us
    unnamed x6, local copies, waits for them, and re-layouts  2.19 us

profile of v2, /device:TPU:6, one launch (start us, length us, event | category | flops | bytes accessed | tf_op | source)
XLA Modules:
  0.0 101.6 jit_solution(15792328544370489926)
XLA Ops:
  0.6 0.0 copy-start.2
  0.6 0.0 copy-start
  0.7 91.1 %shard_map.58 = (f32[512,2048]{1,0:T(8,128)}, f32[832,512]{1,0:T(8,128)S(1)}, f32[8,512]{1,0:T(8,128)S(1)}) custom-call(f32[832,2048]{1,0:T(8,128)} %mom_ref.1, bf16[832,2048]{1,0:T(8,128)(2,1)} %grad_ref.1, f32[2048,512]{1,0:T(8,128)} %rf_hbm.1), custom_call_target="tpu_custom_call" | custom-call | flops 10468982784 | bytes 20971520 | tf_op jit(solution)/shard_map/pallas_call | solution.py:556
  91.8 0.0 copy-done.2
  91.8 0.0 copy-done
  91.8 0.0 copy-start.1
  91.8 2.2 %copy-done.1 = f32[512,2048]{1,0:T(8,128)S(1)} copy-done((f32[512,2048]{1,0:T(8,128)S(1)}, f32[512,2048]{1,0:T(8,128)}, u32[]{:S(2)}) %copy-start.1) | copy-done | bytes 4194328
  94.0 7.7 %shard_map.59 = (f32[832,2048]{1,0:T(8,128)}, f32[2048,512]{1,0:T(8,128)}, f32[832,512]{1,0:T(8,128)}) custom-call(f32[832,2048]{1,0:T(8,128)S(1)} %copy-done, bf16[832,2048]{1,0:T(8,128)(2,1)S(1)} %copy-done.2, f32[832,512]{1,0:T(8,128)S(1)} %get-tuple-element.6.q_ref, f32[512,2048]{1,0:T(8,128)S(1)} %copy-done.1, f32[8,512]{1,0:T(8,128)S(1)} %get-tuple-element.8.scale_ref), custom_call_target="tpu_custom_call" | custom-call | flops 1744830464 | bytes 31457280 | tf_op jit(solution)/shard_map/pallas_call | solution.py:558
Async XLA Ops:
  0.6 91.1 %copy-start.2 = (bf16[832,2048]{1,0:T(8,128)(2,1)S(1)}, bf16[832,2048]{1,0:T(8,128)(2,1)}, u32[]{:S(2)}) copy-start(bf16[832,2048]{1,0:T(8,128)(2,1)} %grad_ref.1) | copy-start | bytes 10223620
  0.6 91.1 %copy-start = (f32[832,2048]{1,0:T(8,128)S(1)}, f32[832,2048]{1,0:T(8,128)}, u32[]{:S(2)}) copy-start(f32[832,2048]{1,0:T(8,128)} %mom_ref.1) | copy-start | bytes 20447236
  91.8 2.2 %copy-start.1 = (f32[512,2048]{1,0:T(8,128)S(1)}, f32[512,2048]{1,0:T(8,128)}, u32[]{:S(2)}) copy-start(f32[512,2048]{1,0:T(8,128)} %get-tuple-element.7.st_ref) | copy-start | bytes 12582916

commit v3 on v2

--- a/solution.py
+++ b/solution.py
@@ -399,9 +399,8 @@
         ltc[0:BK, :] = h
         ltc[BK:2 * BK, :] = l
 
-        @pl.loop(0, N // 256)
-        def _(n_):
-            k = pl.ds(mo(n_ * 256, 256), 256)
+        for n_ in range(N // 1024):
+            k = pl.ds(n_ * 1024, 1024)
             v = dot(ltc[...], bh[:, k])
             tt[g * BK:(g + 1) * BK, k] = v[:BK] + (v[BK:] + dot(ltc[0:BK, :], bl[:, k]))
 
@@ -554,7 +553,7 @@
         cost_estimate=pl.CostEstimate(flops=4 * M * N * R * 3, bytes_accessed=20 << 20, transcendentals=0),
     )
     st, q, scale = big(momentum, gradient, right_factor)
-    tile = 256
+    tile = 512
     return pl.pallas_call(
         last_kernel,
         grid=(N // tile,),

time: 103 us -> 99 us (0.961)
  Pallas kernels: 98.8 us -> 95.2 us
    pallas_call x1, Pallas kernels: 91.1 us -> 88.6 us  [body(): st, q, scale = big(momentum, gradient, right_factor)]
    pallas_call x1, Pallas kernels: 7.66 us -> 6.54 us  [body(): pl.pallas_call(last_kernel, grid=(N // tile,), out_shape=(jax.ShapeDtypeS...]
where the time goes in v3:
time: 99 us; the launch traced here: 98 us
  Pallas kernels  95.2 us (96%)
  local copies, waits for them, and re-layouts  2.19 us (2%)
    pallas_call x1, Pallas kernels, body(): st, q, scale = big(momentum, gradient, right_factor)  88.6 us
    pallas_call x1, Pallas kernels, body(): pl.pallas_call(last_kernel, grid=(N // tile,), out_shape=(jax.ShapeDtypeS...  6.54 us
    unnamed x6, local copies, waits for them, and re-layouts  2.19 us

profile of v3, /device:TPU:6, one launch (start us, length us, event | category | flops | bytes accessed | tf_op | source)
XLA Modules:
  0.0 98.0 jit_solution(4264070997280748167)
XLA Ops:
  0.6 0.0 copy-start.2
  0.6 0.0 copy-start
  0.7 88.6 %shard_map.58 = (f32[512,2048]{1,0:T(8,128)}, f32[832,512]{1,0:T(8,128)S(1)}, f32[8,512]{1,0:T(8,128)S(1)}) custom-call(f32[832,2048]{1,0:T(8,128)} %mom_ref.1, bf16[832,2048]{1,0:T(8,128)(2,1)} %grad_ref.1, f32[2048,512]{1,0:T(8,128)} %rf_hbm.1), custom_call_target="tpu_custom_call" | custom-call | flops 10468982784 | bytes 20971520 | tf_op jit(solution)/shard_map/pallas_call | solution.py:555
  89.3 0.0 copy-done.2
  89.3 0.0 copy-done
  89.3 0.0 copy-start.1
  89.3 2.2 %copy-done.1 = f32[512,2048]{1,0:T(8,128)S(1)} copy-done((f32[512,2048]{1,0:T(8,128)S(1)}, f32[512,2048]{1,0:T(8,128)}, u32[]{:S(2)}) %copy-start.1) | copy-done | bytes 4194328
  91.5 6.5 %shard_map.59 = (f32[832,2048]{1,0:T(8,128)}, f32[2048,512]{1,0:T(8,128)}, f32[832,512]{1,0:T(8,128)}) custom-call(f32[832,2048]{1,0:T(8,128)S(1)} %copy-done, bf16[832,2048]{1,0:T(8,128)(2,1)S(1)} %copy-done.2, f32[832,512]{1,0:T(8,128)S(1)} %get-tuple-element.6.q_ref, f32[512,2048]{1,0:T(8,128)S(1)} %copy-done.1, f32[8,512]{1,0:T(8,128)S(1)} %get-tuple-element.8.scale_ref), custom_call_target="tpu_custom_call" | custom-call | flops 1744830464 | bytes 31457280 | tf_op jit(solution)/shard_map/pallas_call | solution.py:557
Async XLA Ops:
  0.6 88.6 %copy-start.2 = (bf16[832,2048]{1,0:T(8,128)(2,1)S(1)}, bf16[832,2048]{1,0:T(8,128)(2,1)}, u32[]{:S(2)}) copy-start(bf16[832,2048]{1,0:T(8,128)(2,1)} %grad_ref.1) | copy-start | bytes 10223620
  0.6 88.6 %copy-start = (f32[832,2048]{1,0:T(8,128)S(1)}, f32[832,2048]{1,0:T(8,128)}, u32[]{:S(2)}) copy-start(f32[832,2048]{1,0:T(8,128)} %mom_ref.1) | copy-start | bytes 20447236
  89.3 2.2 %copy-start.1 = (f32[512,2048]{1,0:T(8,128)S(1)}, f32[512,2048]{1,0:T(8,128)}, u32[]{:S(2)}) copy-start(f32[512,2048]{1,0:T(8,128)} %get-tuple-element.7.st_ref) | copy-start | bytes 12582916
